TPU v7x, 32 devices: a whole 2x2x4 slice. The times are simulated.
32 devices in a mesh: wide: 8 (over z, x), narrow: 4 (over y, core).
Axes of the slice: x: 2, y: 2, z: 4, core: 2. Of those that a mesh axis runs over, the one named last changes fastest.
Arguments:
- links: float32 [4, 4, 16, 4, 3072], P(None, None, 'wide', 'narrow'), may hold values from -1 to 1, as said below
- gauge: float32 [4, 16, 4, 3072], P(None, 'wide', 'narrow'), may hold values from -1 to 1, as said below
Outputs:
- spectrum: float32 [2, 12, 64, 48, 64], P(None, None, 'wide', 'narrow')
- fixed_gauge: float32 [4, 16, 4, 3072], P(None, 'wide', 'narrow')
Inputs may be any that keep to these rules, and one draw needn't show every extreme that they name: `links`: the four quaternion components of every link form a unit vector, so each link is an SU(2) matrix. `gauge`: the four quaternion components at every site form a unit vector.
All inputs are finite; a program needn't handle non-finite values.
Results may differ from a plain program's by a relative error of at most 0.00015.
Values sent between devices are 32-bit elements; how exact they have to be, the bound alone decides.
A program may use at most 64 MiB of HBM per device.

v0:
```python
import math

import jax
import jax.numpy as jnp
import numpy as np
from jax import lax
from jax.experimental import pallas as pl
from jax.experimental.pallas import tpu as pltpu
from jax.sharding import PartitionSpec as P

LY = 64
LT = 48
HALF_SWEEPS = 2


OMEGA = 1.7


def from_behind(value, axis, steps):
    count = lax.axis_size(axis)
    pairs = [(source, (source + steps) % count) for source in range(count)]
    return lax.ppermute(value, axis, pairs)


def padded_2(block, sides, width):
    for axis, dim in sides:
        count = lax.axis_size(axis)
        forward = [(i, i + 1) for i in range(count - 1)]
        forward.append((count - 1, 0))
        backward = [(target, source) for source, target in forward]
        low = lax.ppermute(
            lax.slice_in_dim(block, block.shape[dim] - width, None, axis=dim), axis, forward
        )
        high = lax.ppermute(lax.slice_in_dim(block, 0, width, axis=dim), axis, backward)
        block = jnp.concatenate([low, block, high], axis=dim)
    return block


def quat_product(first_quat, second_quat):
    scalar = (
        first_quat[0] * second_quat[0]
        - first_quat[1] * second_quat[1]
        - first_quat[2] * second_quat[2]
        - first_quat[3] * second_quat[3]
    )
    vector_one = (
        first_quat[0] * second_quat[1]
        + second_quat[0] * first_quat[1]
        - (first_quat[2] * second_quat[3] - first_quat[3] * second_quat[2])
    )
    vector_two = (
        first_quat[0] * second_quat[2]
        + second_quat[0] * first_quat[2]
        - (first_quat[3] * second_quat[1] - first_quat[1] * second_quat[3])
    )
    vector_three = (
        first_quat[0] * second_quat[3]
        + second_quat[0] * first_quat[3]
        - (first_quat[1] * second_quat[2] - first_quat[2] * second_quat[1])
    )
    return jnp.stack([scalar, vector_one, vector_two, vector_three])


def quat_conj(quaternion):
    return jnp.concatenate([quaternion[:1], -quaternion[1:]], axis=0)


def relax_sites(field, kernel_sum):
    kernel_norm = jnp.sqrt(jnp.sum(kernel_sum * kernel_sum, axis=0))
    rotated = OMEGA * quat_product(quat_conj(kernel_sum), quat_conj(field))
    relaxed = jnp.concatenate(
        [rotated[:1] + (1.0 - OMEGA) * kernel_norm[None], rotated[1:]], axis=0
    )
    relaxed_norm = jnp.sqrt(jnp.sum(relaxed * relaxed, axis=0))
    return quat_product(relaxed, field) / jnp.maximum(relaxed_norm, 1.0)[None]


def site_parity(coord_x, coord_z):
    rows_y = jnp.arange(LY, dtype=jnp.int32)
    rows_t = jnp.arange(LT, dtype=jnp.int32)
    return (
        coord_x[:, None, None, None]
        + coord_z[None, :, None, None]
        + rows_y[None, None, :, None]
        + rows_t[None, None, None, :]
    ) % 2


def fourier_tables(length):
    indices = jnp.arange(length, dtype=jnp.int32)
    phases = indices[:, None] * indices[None, :] % length
    angles = phases.astype(jnp.float32) * (2.0 * math.pi / length)
    return (jnp.cos(angles), jnp.sin(angles))


def along_axis(spectrum, axis_number):
    cosine, sine_part = fourier_tables(spectrum.shape[axis_number])
    moved_last = jnp.moveaxis(spectrum, axis_number, -1)
    cos_term = jnp.matmul(moved_last, cosine, precision=lax.Precision.HIGHEST)
    sin_term = jnp.matmul(moved_last, sine_part, precision=lax.Precision.HIGHEST)
    rotated = jnp.stack([cos_term[0] + sin_term[1], cos_term[1] - sin_term[0]])
    return jnp.moveaxis(rotated, -1, axis_number)


def along_x(spectrum):
    return along_axis(spectrum, 2)


def along_z(spectrum):
    return along_axis(spectrum, 3)


def body(links, gauge):
    slab_x = gauge.shape[1]
    slab_z = gauge.shape[2]
    count_wide = lax.axis_size("wide")
    count_narrow = lax.axis_size("narrow")
    coord_x = lax.axis_index("wide") * slab_x + jnp.arange(slab_x, dtype=jnp.int32)
    coord_z = lax.axis_index("narrow") * slab_z + jnp.arange(slab_z, dtype=jnp.int32)
    link = links.reshape((4, 4, slab_x, slab_z, LY, LT))
    field = gauge.reshape((4, slab_x, slab_z, LY, LT))
    parity = site_parity(coord_x, coord_z)
    from_below_x = from_behind(link[:, 0, slab_x - 1 :], "wide", 1)
    from_below_z = from_behind(link[:, 2, :, slab_z - 1 :], "narrow", 1)
    behind_links = [
        jnp.concatenate([from_below_x, link[:, 0, : slab_x - 1]], axis=1),
        jnp.roll(link[:, 1], 1, axis=3),
        jnp.concatenate([from_below_z, link[:, 2, :, : slab_z - 1]], axis=2),
        jnp.roll(link[:, 3], 1, axis=4),
    ]
    for half_sweep in range(HALF_SWEEPS):
        update_side = half_sweep % 2
        padded = padded_2(field, (("wide", 1), ("narrow", 2)), 1)
        center = padded[:, 1:-1, 1:-1]
        ahead_list = [
            padded[:, 2:, 1:-1],
            jnp.roll(center, -1, axis=3),
            padded[:, 1:-1, 2:],
            jnp.roll(center, -1, axis=4),
        ]
        behind_list = [
            padded[:, :-2, 1:-1],
            jnp.roll(center, 1, axis=3),
            padded[:, 1:-1, :-2],
            jnp.roll(center, 1, axis=4),
        ]
        kernel_sum = jnp.zeros(field.shape, jnp.float32)
        for direction in range(4):
            kernel_sum = (
                kernel_sum
                + quat_product(link[:, direction], quat_conj(ahead_list[direction]))
                + quat_product(
                    quat_conj(behind_links[direction]), quat_conj(behind_list[direction])
                )
            )
        field = jnp.where((parity == update_side)[None], relax_sites(field, kernel_sum), field)
    next_x = from_behind(field[:, :1], "wide", -1)
    next_z = from_behind(field, "narrow", -1)
    forward_list = [
        jnp.concatenate([field[:, 1:], next_x], axis=1),
        jnp.roll(field, -1, axis=3),
        jnp.concatenate([field[:, :, 1:], next_z], axis=2),
        jnp.roll(field, -1, axis=4),
    ]
    pieces = []
    for direction in range(4):
        transformed = quat_product(
            quat_product(field, link[:, direction]), quat_conj(forward_list[direction])
        )
        pieces.append(transformed[1:])
    potential = jnp.stack(pieces, axis=1).reshape((12, slab_x, slab_z, LY, LT))
    cosine_t, sine_t = fourier_tables(LT)
    real_part = jnp.matmul(potential, cosine_t, precision=lax.Precision.HIGHEST)
    imag_part = -jnp.matmul(potential, sine_t, precision=lax.Precision.HIGHEST)
    spectrum = along_axis(jnp.stack([real_part, imag_part]), 4)
    spectrum = along_x(lax.all_to_all(spectrum, "wide", split_axis=4, concat_axis=2, tiled=True))
    spectrum = along_z(lax.all_to_all(spectrum, "narrow", split_axis=5, concat_axis=3, tiled=True))
    scale = float(count_wide * slab_x * count_narrow * slab_z * LY * LT) ** (-0.5)
    spectrum = spectrum * scale
    full_x = spectrum.shape[2]
    full_z = spectrum.shape[3]
    spectrum = jnp.transpose(spectrum, (0, 1, 4, 5, 2, 3))
    spectrum = spectrum.reshape((2, 12, spectrum.shape[2], spectrum.shape[3], full_x * full_z))
    return (spectrum, field.reshape((4, slab_x, slab_z, LY * LT)))


ROWS = 8
INNER = LY // ROWS
LANES = INNER * LT
COMPS = 12
MESH = pl.DeviceIdType.MESH


def split_pair(table):
    high = table.astype(jnp.bfloat16)
    low = (table - high.astype(np.float32)).astype(jnp.bfloat16)
    return np.stack([np.asarray(high), np.asarray(low)])


def make_tables(wide, narrow, slab_x):
    turn = 2.0 * np.pi
    per_kt = LT // narrow
    k0 = np.arange(ROWS)
    angle = turn * (np.outer(k0, k0) % ROWS) / ROWS
    first = np.zeros((2, 16, ROWS, COMPS, ROWS))
    for c in range(COMPS):
        first[0, c, :, c, :] = np.cos(angle)
        first[1, c, :, c, :] = -np.sin(angle)
    first = first.reshape(256, COMPS * ROWS)
    inner = np.repeat(np.arange(INNER), LT)
    angle = turn * np.outer(k0, inner) / LY
    twiddle = np.stack([np.cos(angle), np.sin(angle)])
    time = np.tile(np.arange(LT), INNER)
    kb = np.arange(wide)
    kt = np.arange(LT)
    part_b = np.exp(-1j * turn * (np.outer(kb, inner) % wide) / wide)
    part_t = np.exp(-1j * turn * (np.outer(kt, time) % LT) / LT)
    phase = (part_b[:, None, :] * part_t[None]).reshape(wide, narrow, per_kt, LANES)
    second = np.empty((wide, narrow, 2, per_kt, 2, LANES))
    second[:, :, 0, :, 0] = phase.real
    second[:, :, 0, :, 1] = -phase.imag
    second[:, :, 1, :, 0] = phase.imag
    second[:, :, 1, :, 1] = phase.real
    second = second.reshape(wide * narrow * 2 * per_kt, 2 * LANES)
    nx = wide * slab_x
    kx = np.arange(nx)
    kz = np.arange(narrow)
    part_x = np.exp(-1j * turn * (np.outer(kx, kx) % nx) / nx).reshape(nx, wide, slab_x)
    part_z = np.exp(-1j * turn * (np.outer(kz, kz) % narrow) / narrow)
    phase = part_x[:, None, :, None, :] * part_z[None, :, None, :, None]
    phase = phase * float(nx * narrow * LY * LT) ** (-0.5)
    third = np.empty((2, nx, narrow, wide, narrow, slab_x, 2))
    third[0, ..., 0] = phase.real
    third[0, ..., 1] = -phase.imag
    third[1, ..., 0] = phase.imag
    third[1, ..., 1] = phase.real
    third = third.reshape(2 * nx * narrow, wide * narrow * slab_x * 2)
    f32 = np.float32
    return (
        split_pair(first.astype(f32)),
        twiddle.astype(f32),
        split_pair(second.astype(f32)),
        split_pair(third.astype(f32)),
    )


def qmul(a, b):
    return [
        a[0] * b[0] - a[1] * b[1] - a[2] * b[2] - a[3] * b[3],
        a[0] * b[1] + b[0] * a[1] - (a[2] * b[3] - a[3] * b[2]),
        a[0] * b[2] + b[0] * a[2] - (a[3] * b[1] - a[1] * b[3]),
        a[0] * b[3] + b[0] * a[3] - (a[1] * b[2] - a[2] * b[1]),
    ]


def qconj(a):
    return [a[0], -a[1], -a[2], -a[3]]


def qadd(a, b):
    return [p + q for p, q in zip(a, b)]


def qwhere(mask, a, b):
    return [jnp.where(mask, p, q) for p, q in zip(a, b)]


def qnorm(a):
    return jnp.sqrt(a[0] * a[0] + a[1] * a[1] + a[2] * a[2] + a[3] * a[3])


def halves(value):
    high = value.astype(jnp.bfloat16)
    return high, (value - high.astype(jnp.float32)).astype(jnp.bfloat16)


def dot3(pair_a, pair_b, dims):
    def one(a, b):
        return lax.dot_general(a, b, (dims, ((), ())), preferred_element_type=jnp.float32)

    return one(pair_a[0], pair_b[0]) + (one(pair_a[1], pair_b[0]) + one(pair_a[0], pair_b[1]))


def fused(
    wide, narrow,
    links_ref, gauge_ref, first_ref, twiddle_ref, second_hbm, third_ref,
    out_ref, field_ref,
    second_ref, face_out, face_in, pot, outgoing, arrived, turned,
    table_sem, face_send, face_recv, far_send, far_recv, own_sem,
):
    my_w = lax.axis_index("wide")
    my_n = lax.axis_index("narrow")
    per_kt = LT // narrow
    block = 4 * per_kt
    table_copy = pltpu.make_async_copy(second_hbm, second_ref, table_sem)
    table_copy.start()

    barrier = pltpu.get_barrier_semaphore()
    for i in range(wide):
        for k in range(narrow):
            if i or k:
                peer = (lax.rem(my_w + i, wide), lax.rem(my_n + k, narrow))
                pl.semaphore_signal(barrier, inc=1, device_id=peer, device_id_type=MESH)

    lane = lax.broadcasted_iota(jnp.int32, (ROWS, LANES), 1)
    inner = jnp.zeros((ROWS, LANES), jnp.int32)
    for j in range(1, INNER):
        inner = inner + jnp.where(lane >= LT * j, 1, 0)
    time = lane - LT * inner
    even = ((my_n + inner + time) & 1) == 0
    odd = jnp.logical_not(even)
    first_t, last_t = time == 0, time == LT - 1
    first_j, last_j = inner == 0, inner == INNER - 1

    def ahead_t(v):
        return jnp.where(last_t, pltpu.roll(v, LT - 1, 1), pltpu.roll(v, LANES - 1, 1))

    def behind_t(v):
        return jnp.where(first_t, pltpu.roll(v, LANES - LT + 1, 1), pltpu.roll(v, 1, 1))

    def ahead_y(v):
        moved = pltpu.roll(v, LANES - LT, 1)
        return jnp.where(last_j, pltpu.roll(moved, ROWS - 1, 0), moved)

    def behind_y(v):
        moved = pltpu.roll(v, LT, 1)
        return jnp.where(first_j, pltpu.roll(moved, 1, 0), moved)

    def tile(ref, index):
        return jnp.concatenate(
            [ref[pl.ds(index * 24 + s, ROWS, stride=3), :] for s in range(3)], axis=1
        )

    def both(ref, index_zero):
        zero, one = tile(ref, index_zero), tile(ref, index_zero + 1)
        return jnp.where(even, zero, one), jnp.where(even, one, zero)

    link = [[None] * 4, [None] * 4]
    for mu in range(4):
        pairs = [both(links_ref, (a * 4 + mu) * 2) for a in range(4)]
        for p in range(2):
            link[p][mu] = [pair[p] for pair in pairs]
    pairs = [both(gauge_ref, a * 2) for a in range(4)]
    field = [[pair[p] for pair in pairs] for p in range(2)]

    def neighbour(step_w, step_n):
        return (
            lax.rem(my_w + step_w + wide, wide),
            lax.rem(my_n + step_n + narrow, narrow),
        )

    def send_face(source, slot, step_w, step_n):
        copy = pltpu.make_async_remote_copy(
            src_ref=face_out.at[source],
            dst_ref=face_in.at[slot],
            send_sem=face_send.at[slot],
            recv_sem=face_recv.at[slot],
            device_id=neighbour(step_w, step_n),
            device_id_type=MESH,
        )
        copy.start()
        return copy

    def put_face(source, value):
        for a in range(4):
            face_out[source, a] = value[a]

    def got_face(slot):
        return [face_in[slot, a] for a in range(4)]

    copies = []
    moved_links = None
    kept_x = kept_z = None
    for half in range(HALF_SWEEPS):
        p = half % 2
        here = even if p == 0 else odd
        other = field[1 - p]
        moved_links = [qmul(other, link[1 - p][mu]) for mu in range(4)]
        put_face(3 * half, other)
        put_face(3 * half + 1, moved_links[0])
        put_face(3 * half + 2, moved_links[2])
        if half == 0:
            pl.semaphore_wait(barrier, wide * narrow - 1)
        started = [
            send_face(3 * half, 4 * half, -1, 0),
            send_face(3 * half, 4 * half + 1, 0, -1),
            send_face(3 * half + 1, 4 * half + 2, 1, 0),
            send_face(3 * half + 2, 4 * half + 3, 0, 1),
        ]
        copies += started
        total = qmul([ahead_y(v) for v in other], qconj(link[p][1]))
        total = qadd(total, [behind_y(v) for v in moved_links[1]])
        total = qadd(total, qmul([ahead_t(v) for v in other], qconj(link[p][3])))
        total = qadd(total, [behind_t(v) for v in moved_links[3]])
        for copy in started:
            copy.wait_recv()
        kept_x, kept_z = got_face(4 * half), got_face(4 * half + 1)
        total = qadd(total, qmul(qwhere(here, other, kept_x), qconj(link[p][0])))
        total = qadd(total, qmul(kept_z, qconj(link[p][2])))
        total = qadd(total, qwhere(here, got_face(4 * half + 2), moved_links[0]))
        total = qadd(total, got_face(4 * half + 3))
        centre = field[p]
        relaxed = [OMEGA * v for v in qmul(total, qconj(centre))]
        relaxed[0] = relaxed[0] + (1.0 - OMEGA) * qnorm(total)
        bound = jnp.maximum(qnorm(relaxed), 1.0)
        field[p] = [v / bound for v in qmul(relaxed, centre)]

    p = (HALF_SWEEPS - 1) % 2
    source, slot = 3 * HALF_SWEEPS, 4 * HALF_SWEEPS
    put_face(source, field[p])
    started = [send_face(source, slot, -1, 0), send_face(source, slot + 1, 0, -1)]
    copies += started
    for a in range(4):
        zero = jnp.where(even, field[0][a], field[1][a])
        one = jnp.where(even, field[1][a], field[0][a])
        for x, value in enumerate((zero, one)):
            for s in range(3):
                field_ref[pl.ds((a * 2 + x) * 24 + s, ROWS, stride=3), :] = value[
                    :, 128 * s : 128 * (s + 1)
                ]
    carried = [None, None]
    carried[1 - p] = moved_links
    carried[p] = [qmul(field[p], link[p][mu]) for mu in range(4)]
    here = even if p == 0 else odd

    def put_potential(mu, ahead):
        value = [qmul(carried[q][mu], qconj(ahead[q])) for q in range(2)]
        for a in range(3):
            c = 4 * a + mu
            zero = jnp.where(even, value[0][a + 1], value[1][a + 1])
            one = jnp.where(even, value[1][a + 1], value[0][a + 1])
            pot[0, c * ROWS : (c + 1) * ROWS, :] = zero
            pot[1, c * ROWS : (c + 1) * ROWS, :] = one

    put_potential(1, [[ahead_y(v) for v in field[1 - q]] for q in range(2)])
    put_potential(3, [[ahead_t(v) for v in field[1 - q]] for q in range(2)])
    for copy in started:
        copy.wait_recv()
    fresh_x, fresh_z = got_face(slot), got_face(slot + 1)
    there = odd if p == 0 else even
    ahead = [None, None]
    ahead[p] = qwhere(here, field[1 - p], kept_x)
    ahead[1 - p] = qwhere(there, field[p], fresh_x)
    put_potential(0, ahead)
    ahead[p], ahead[1 - p] = kept_z, fresh_z
    put_potential(2, ahead)

    first = (first_ref[0], first_ref[1])
    cosine, sine = twiddle_ref[0][None], twiddle_ref[1][None]
    highs, lows = [], []
    for x in range(2):
        turned_r = dot3(first, halves(pot[x]), ((1,), (0,))).reshape(2, 16, ROWS, LANES)
        real = turned_r[0] * cosine + turned_r[1] * sine
        imag = turned_r[1] * cosine - turned_r[0] * sine
        both_parts = jnp.concatenate(
            [real.reshape(128, LANES), imag.reshape(128, LANES)], axis=1
        )
        high, low = halves(both_parts)
        highs.append(high)
        lows.append(low)
    mid = (jnp.concatenate(highs, axis=0), jnp.concatenate(lows, axis=0))
    table_copy.wait()
    per_b = narrow * 2 * per_kt
    group = 2
    for g in range(wide // group):
        rows = slice(g * group * per_b, (g + 1) * group * per_b)
        value = dot3((second_ref[0, rows, :], second_ref[1, rows, :]), mid, ((1,), (1,)))
        for m in range(group * narrow):
            target = g * group * narrow + m
            for x in range(2):
                outgoing[target * block + x * 2 * per_kt : target * block + (x + 1) * 2 * per_kt, :] = (
                    value[m * 2 * per_kt : (m + 1) * 2 * per_kt, 128 * x : 128 * (x + 1)]
                )

    def span(w, n):
        return pl.ds(pl.multiple_of((w * narrow + n) * block, 8), block)

    mine = span(my_w, my_n)
    for i in range(wide):
        for k in range(narrow):
            if i or k:
                w, n = lax.rem(my_w + i, wide), lax.rem(my_n + k, narrow)
                copy = pltpu.make_async_remote_copy(
                    src_ref=outgoing.at[span(w, n)],
                    dst_ref=arrived.at[mine],
                    send_sem=far_send.at[i * narrow + k],
                    recv_sem=far_recv.at[i * narrow + k],
                    device_id=(w, n),
                    device_id_type=MESH,
                )
                copy.start()
                copies.append(copy)
    own = pltpu.make_async_copy(outgoing.at[mine], arrived.at[mine], own_sem)
    own.start()
    own.wait()
    for i in range(wide):
        for k in range(narrow):
            if i or k:
                w, n = lax.rem(my_w + wide - i, wide), lax.rem(my_n + narrow - k, narrow)
                pltpu.make_async_remote_copy(
                    src_ref=outgoing.at[span(w, n)],
                    dst_ref=arrived.at[span(w, n)],
                    send_sem=far_send.at[i * narrow + k],
                    recv_sem=far_recv.at[i * narrow + k],
                    device_id=(w, n),
                    device_id_type=MESH,
                ).wait_recv()

    third = (third_ref[0], third_ref[1])
    momenta = third_ref.shape[1] // 2
    depth = third_ref.shape[2]
    for kt in range(per_kt):
        value = halves(arrived[pl.ds(kt, depth, stride=per_kt), :])
        turned[kt * 128 : (kt + 1) * 128, :] = dot3(third, value, ((1,), (0,))).T
    for c in range(COMPS):
        for k0 in range(ROWS):
            value = turned[pl.ds(c * ROWS + k0, per_kt, stride=128), :]
            out_ref[0, c, k0] = value[:, :momenta]
            out_ref[1, c, k0] = value[:, momenta:]
    for copy in copies:
        copy.wait_send()


def fused_body(wide, narrow, links, gauge):
    slab_x = gauge.shape[1]
    tables = make_tables(wide, narrow, slab_x)
    devices = wide * narrow
    per_kt = LT // narrow
    block = 4 * per_kt
    faces = 4 * HALF_SWEEPS + 2
    vmem = pl.BlockSpec(memory_space=pltpu.VMEM)
    spectrum, field = pl.pallas_call(
        lambda *refs: fused(wide, narrow, *refs),
        out_shape=(
            jax.ShapeDtypeStruct((2, COMPS, ROWS, per_kt, wide * slab_x * narrow), jnp.float32),
            jax.ShapeDtypeStruct((4 * slab_x * 24, 128), jnp.float32),
        ),
        in_specs=[vmem, vmem, vmem, vmem, pl.BlockSpec(memory_space=pl.ANY), vmem],
        out_specs=(vmem, vmem),
        scratch_shapes=[
            pltpu.VMEM(tables[2].shape, jnp.bfloat16),
            pltpu.VMEM((3 * HALF_SWEEPS + 1, 4, ROWS, LANES), jnp.float32),
            pltpu.VMEM((faces, 4, ROWS, LANES), jnp.float32),
            pltpu.VMEM((2, COMPS * ROWS, LANES), jnp.float32),
            pltpu.VMEM((devices * block, 128), jnp.float32),
            pltpu.VMEM((devices * block, 128), jnp.float32),
            pltpu.VMEM((per_kt * 128, 128), jnp.float32),
            pltpu.SemaphoreType.DMA,
            pltpu.SemaphoreType.DMA((faces,)),
            pltpu.SemaphoreType.DMA((faces,)),
            pltpu.SemaphoreType.DMA((devices,)),
            pltpu.SemaphoreType.DMA((devices,)),
            pltpu.SemaphoreType.DMA,
        ],
        compiler_params=pltpu.CompilerParams(
            collective_id=0, has_side_effects=True, vmem_limit_bytes=40 * 1024 * 1024
        ),
    )(
        links.reshape(4 * 4 * slab_x * 24, 128),
        gauge.reshape(4 * slab_x * 24, 128),
        *[jnp.asarray(table) for table in tables],
    )
    return spectrum, field.reshape(gauge.shape)


def solution(mesh):
    in_specs = (P(None, None, "wide", "narrow", None), P(None, "wide", "narrow", None))
    out_specs = (P(None, None, "wide", "narrow", None), P(None, "wide", "narrow", None))
    wide, narrow = mesh.shape["wide"], mesh.shape["narrow"]

    def per_device(links, gauge):
        slab_x, slab_z = gauge.shape[1:3]
        fits = slab_x == 2 and slab_z == 1 and wide * ROWS == LY and wide * narrow * 4 == 128
        if fits:
            return fused_body(wide, narrow, links, gauge)
        return body(links, gauge)

    return jax.shard_map(
        per_device, mesh=mesh, in_specs=in_specs, out_specs=out_specs, check_vma=False
    )
```

profile of v0, /device:TPU:11, one launch (start us, length us, event | category | flops | bytes accessed | tf_op | source)
XLA Modules:
  0.0 47.9 jit_solution(12023295154333630642)
XLA Ops:
  0.6 0.0 copy-start
  0.6 1.7 %copy-done = bf16[2,768,768]{2,1,0:T(8,128)(2,1)S(1)} copy-done((bf16[2,768,768]{2,1,0:T(8,128)(2,1)S(1)}, bf16[2,768,768]{2,1,0:T(8,128)(2,1)}, u32[]{:S(2)}) %copy-start) | copy-done | bytes 2359320
  2.3 0.0 copy-start.1
  2.3 1.0 %copy-done.1 = f32[4,4,2,1,3072]{4,3,2,1,0:T(1,128)S(1)} copy-done((f32[4,4,2,1,3072]{4,3,2,1,0:T(1,128)S(1)}, f32[4,4,2,1,3072]{4,3,2,1,0:T(1,128)}, u32[]{:S(2)}) %copy-start.1) | copy-done | bytes 393240
  3.3 0.0 copy-start.2
  3.3 0.9 %copy-done.2 = bf16[2,256,96]{2,1,0:T(8,128)(2,1)S(1)} copy-done((bf16[2,256,96]{2,1,0:T(8,128)(2,1)S(1)}, bf16[2,256,96]{2,1,0:T(8,128)(2,1)}, u32[]{:S(2)}) %copy-start.2) | copy-done | bytes 98328
  4.2 0.0 copy-start.3
  4.2 0.9 %copy-done.3 = f32[4,2,1,3072]{3,2,1,0:T(1,128)S(1)} copy-done((f32[4,2,1,3072]{3,2,1,0:T(1,128)S(1)}, f32[4,2,1,3072]{3,2,1,0:T(1,128)}, u32[]{:S(2)}) %copy-start.3) | copy-done | bytes 98328
  5.1 0.0 copy-start.4
  5.1 0.8 %copy-done.4 = bf16[2,128,128]{2,1,0:T(8,128)(2,1)S(1)} copy-done((bf16[2,128,128]{2,1,0:T(8,128)(2,1)S(1)}, bf16[2,128,128]{2,1,0:T(8,128)(2,1)}, u32[]{:S(2)}) %copy-start.4) | copy-done | bytes 65560
  5.9 0.0 copy-start.5
  5.9 0.7 %copy-done.5 = f32[2,8,384]{2,1,0:T(8,128)S(1)} copy-done((f32[2,8,384]{2,1,0:T(8,128)S(1)}, f32[2,8,384]{2,1,0:T(8,128)}, u32[]{:S(2)}) %copy-start.5) | copy-done | bytes 24600
  6.7 39.1 %shard_map.77 = (f32[2,12,8,12,64]{4,3,2,1,0:T(8,128)S(1)}, f32[192,128]{1,0:T(8,128)S(1)}) custom-call(f32[768,128]{1,0:T(8,128)S(1)} %bitcast.3, f32[192,128]{1,0:T(8,128)S(1)} %bitcast.4, bf16[2,256,96]{2,1,0:T(8,128)(2,1)S(1)} %copy-done.2, f32[2,8,384]{2,1,0:T(8,128)S(1)} %copy-done.5, bf16[2,768,768]{2,1,0:T(8,128)(2,1)S(1)} %copy-done, ...), custom_call_target="tpu_custom_call" | custom-call | tf_op jit(solution)/shard_map/pallas_call | solution.py:532
  45.8 1.5 %copy.8 = f32[2,12,8,12,64]{4,2,3,1,0:T(8,128)} copy(f32[2,12,8,12,64]{4,3,2,1,0:T(8,128)S(1)} %get-tuple-element.6) | data formatting | bytes 1179648
  47.3 0.6 %copy.11 = f32[4,2,1,3072]{3,2,1,0:T(1,128)} copy(f32[4,2,1,3072]{3,2,1,0:T(1,128)S(1)} %bitcast.5) | data formatting | bytes 196608
Async XLA Ops:
  0.6 1.7 %copy-start = (bf16[2,768,768]{2,1,0:T(8,128)(2,1)S(1)}, bf16[2,768,768]{2,1,0:T(8,128)(2,1)}, u32[]{:S(2)}) copy-start(bf16[2,768,768]{2,1,0:T(8,128)(2,1)} %constant.10.clone.refs_4_) | copy-start | bytes 7077892
  2.3 1.0 %copy-start.1 = (f32[4,4,2,1,3072]{4,3,2,1,0:T(1,128)S(1)}, f32[4,4,2,1,3072]{4,3,2,1,0:T(1,128)}, u32[]{:S(2)}) copy-start(f32[4,4,2,1,3072]{4,3,2,1,0:T(1,128)} %param.6) | copy-start | bytes 1179652
  3.3 0.9 %copy-start.2 = (bf16[2,256,96]{2,1,0:T(8,128)(2,1)S(1)}, bf16[2,256,96]{2,1,0:T(8,128)(2,1)}, u32[]{:S(2)}) copy-start(bf16[2,256,96]{2,1,0:T(8,128)(2,1)} %constant.8.clone.refs_2_) | copy-start | bytes 294916
  4.2 0.9 %copy-start.3 = (f32[4,2,1,3072]{3,2,1,0:T(1,128)S(1)}, f32[4,2,1,3072]{3,2,1,0:T(1,128)}, u32[]{:S(2)}) copy-start(f32[4,2,1,3072]{3,2,1,0:T(1,128)} %param.7) | copy-start | bytes 294916
  5.1 0.8 %copy-start.4 = (bf16[2,128,128]{2,1,0:T(8,128)(2,1)S(1)}, bf16[2,128,128]{2,1,0:T(8,128)(2,1)}, u32[]{:S(2)}) copy-start(bf16[2,128,128]{2,1,0:T(8,128)(2,1)} %constant.11.clone.refs_5_) | copy-start | bytes 196612
  5.9 0.7 %copy-start.5 = (f32[2,8,384]{2,1,0:T(8,128)S(1)}, f32[2,8,384]{2,1,0:T(8,128)}, u32[]{:S(2)}) copy-start(f32[2,8,384]{2,1,0:T(8,128)} %constant.9.clone.refs_3_) | copy-start | bytes 73732
where the time goes:
time: 48.3 us; the launch traced here: 47.9 us
  Pallas kernels  39.1 us (81%)
  local copies, waits for them, and re-layouts  8.14 us (17%)
  between operations  0.65 us (1%)
    pallas_call x1, Pallas kernels, fused_body(): pl.pallas_call(lambda *refs: fused(wide, narrow, *refs), out_shape=(jax.S...  39.1 us
    unnamed x14, local copies, waits for them, and re-layouts  8.14 us

commit v1 on v0

--- a/solution.py
+++ b/solution.py
@@ -188,6 +188,7 @@
 INNER = LY // ROWS
 LANES = INNER * LT
 COMPS = 12
+VMEM_MIB = 60
 MESH = pl.DeviceIdType.MESH
 
 
@@ -221,7 +222,7 @@
     second[:, :, 0, :, 1] = -phase.imag
     second[:, :, 1, :, 0] = phase.imag
     second[:, :, 1, :, 1] = phase.real
-    second = second.reshape(wide * narrow * 2 * per_kt, 2 * LANES)
+    second = second.transpose(0, 2, 1, 3, 4, 5).reshape(wide * narrow * 2 * per_kt, 2 * LANES)
     nx = wide * slab_x
     kx = np.arange(nx)
     kz = np.arange(narrow)
@@ -234,7 +235,7 @@
     third[0, ..., 1] = -phase.imag
     third[1, ..., 0] = phase.imag
     third[1, ..., 1] = phase.real
-    third = third.reshape(2 * nx * narrow, wide * narrow * slab_x * 2)
+    third = third.transpose(0, 1, 2, 5, 6, 3, 4).reshape(2 * nx * narrow, wide * narrow * slab_x * 2)
     f32 = np.float32
     return (
         split_pair(first.astype(f32)),
@@ -283,17 +284,30 @@
 
 def fused(
     wide, narrow,
-    links_ref, gauge_ref, first_ref, twiddle_ref, second_hbm, third_ref,
+    links_hbm, gauge_hbm, first_hbm, twiddle_hbm, second_hbm, third_hbm,
     out_ref, field_ref,
-    second_ref, face_out, face_in, pot, outgoing, arrived, turned,
-    table_sem, face_send, face_recv, far_send, far_recv, own_sem,
+    links_ref, gauge_ref, first_ref, twiddle_ref, second_ref, third_ref,
+    face_out, face_in, pot, outgoing, arrived,
+    load_sem, face_send, face_recv, far_send, far_recv, own_sem,
 ):
     my_w = lax.axis_index("wide")
     my_n = lax.axis_index("narrow")
     per_kt = LT // narrow
-    block = 4 * per_kt
-    table_copy = pltpu.make_async_copy(second_hbm, second_ref, table_sem)
-    table_copy.start()
+    loads = [
+        pltpu.make_async_copy(source, target, load_sem.at[i])
+        for i, (source, target) in enumerate(
+            [
+                (links_hbm, links_ref),
+                (gauge_hbm, gauge_ref),
+                (first_hbm, first_ref),
+                (twiddle_hbm, twiddle_ref),
+                (third_hbm, third_ref),
+                (second_hbm, second_ref),
+            ]
+        )
+    ]
+    for load in loads:
+        load.start()
 
     barrier = pltpu.get_barrier_semaphore()
     for i in range(wide):
@@ -335,6 +349,8 @@
         zero, one = tile(ref, index_zero), tile(ref, index_zero + 1)
         return jnp.where(even, zero, one), jnp.where(even, one, zero)
 
+    loads[0].wait()
+    loads[1].wait()
     link = [[None] * 4, [None] * 4]
     for mu in range(4):
         pairs = [both(links_ref, (a * 4 + mu) * 2) for a in range(4)]
@@ -445,6 +461,8 @@
     ahead[p], ahead[1 - p] = kept_z, fresh_z
     put_potential(2, ahead)
 
+    loads[2].wait()
+    loads[3].wait()
     first = (first_ref[0], first_ref[1])
     cosine, sine = twiddle_ref[0][None], twiddle_ref[1][None]
     highs, lows = [], []
@@ -458,67 +476,112 @@
         high, low = halves(both_parts)
         highs.append(high)
         lows.append(low)
-    mid = (jnp.concatenate(highs, axis=0), jnp.concatenate(lows, axis=0))
-    table_copy.wait()
-    per_b = narrow * 2 * per_kt
-    group = 2
-    for g in range(wide // group):
-        rows = slice(g * group * per_b, (g + 1) * group * per_b)
-        value = dot3((second_ref[0, rows, :], second_ref[1, rows, :]), mid, ((1,), (1,)))
-        for m in range(group * narrow):
-            target = g * group * narrow + m
-            for x in range(2):
-                outgoing[target * block + x * 2 * per_kt : target * block + (x + 1) * 2 * per_kt, :] = (
-                    value[m * 2 * per_kt : (m + 1) * 2 * per_kt, 128 * x : 128 * (x + 1)]
-                )
+    used = COMPS * ROWS
+    over = 128 - used
+
+    def arrange(parts):
+        zeros = jnp.zeros((over, 2 * LANES), jnp.bfloat16)
+        return jnp.concatenate(
+            [parts[0][:used], parts[1][:over], zeros, parts[1][over:used], zeros], axis=0
+        )
+
+    mid = (arrange(highs), arrange(lows))
+    loads[5].wait()
+    per_b = narrow * per_kt
+    pair = 2
+    groups = wide // pair
+    block = message_rows(per_kt)
+    my_z, my_x = my_w // pair, lax.rem(my_w, pair)
 
     def span(w, n):
         return pl.ds(pl.multiple_of((w * narrow + n) * block, 8), block)
 
     mine = span(my_w, my_n)
-    for i in range(wide):
-        for k in range(narrow):
-            if i or k:
-                w, n = lax.rem(my_w + i, wide), lax.rem(my_n + k, narrow)
+    steps = sorted(range(groups), key=lambda step: -min(step, groups - step))
+    own = None
+    for place, step in enumerate(steps):
+        group = lax.rem(my_z + step, groups)
+        rows = pl.ds(pl.multiple_of(group * (pair * 2 * per_b), 16), pair * 2 * per_b)
+        value = dot3((second_ref[0, rows, :], second_ref[1, rows, :]), mid, ((1,), (1,)))
+        for q in range(pair):
+            real = value[q * 2 * per_b : q * 2 * per_b + per_b]
+            imag = value[q * 2 * per_b + per_b : (q + 1) * 2 * per_b]
+            extra = real[:, 128:] + pltpu.roll(imag[:, 128:], 64, 1)
+            for n in range(narrow):
+                base = ((place * pair + q) * narrow + n) * block
+                take = slice(n * per_kt, (n + 1) * per_kt)
+                outgoing[base : base + per_kt, :] = real[take, :128]
+                outgoing[base + per_kt : base + 2 * per_kt, :] = imag[take, :128]
+                outgoing[base + 2 * per_kt : base + 3 * per_kt, :] = extra[take]
+                outgoing[base + 3 * per_kt : base + block, :] = jnp.zeros(
+                    (block - 3 * per_kt, 128), jnp.float32
+                )
+        for q in range(pair):
+            x = lax.rem(my_x + q, pair)
+            for k in range(narrow):
+                w, n = group * pair + x, lax.rem(my_n + k, narrow)
+                index = (step * pair + q) * narrow + k
+                held = pl.ds(
+                    pl.multiple_of(((place * pair + x) * narrow + n) * block, 8), block
+                )
+                if index == 0:
+                    own = pltpu.make_async_copy(outgoing.at[held], arrived.at[mine], own_sem)
+                    own.start()
+                    continue
                 copy = pltpu.make_async_remote_copy(
-                    src_ref=outgoing.at[span(w, n)],
+                    src_ref=outgoing.at[held],
                     dst_ref=arrived.at[mine],
-                    send_sem=far_send.at[i * narrow + k],
-                    recv_sem=far_recv.at[i * narrow + k],
+                    send_sem=far_send.at[index],
+                    recv_sem=far_recv.at[index],
                     device_id=(w, n),
                     device_id_type=MESH,
                 )
                 copy.start()
                 copies.append(copy)
-    own = pltpu.make_async_copy(outgoing.at[mine], arrived.at[mine], own_sem)
-    own.start()
     own.wait()
-    for i in range(wide):
-        for k in range(narrow):
-            if i or k:
-                w, n = lax.rem(my_w + wide - i, wide), lax.rem(my_n + narrow - k, narrow)
+    loads[4].wait()
+    for step in range(groups):
+        for q in range(pair):
+            for k in range(narrow):
+                index = (step * pair + q) * narrow + k
+                if index == 0:
+                    continue
+                w = lax.rem(my_z + groups - step, groups) * pair + lax.rem(my_x + q, pair)
+                n = lax.rem(my_n + narrow - k, narrow)
                 pltpu.make_async_remote_copy(
-                    src_ref=outgoing.at[span(w, n)],
+                    src_ref=outgoing.at[pl.ds(0, block)],
                     dst_ref=arrived.at[span(w, n)],
-                    send_sem=far_send.at[i * narrow + k],
-                    recv_sem=far_recv.at[i * narrow + k],
+                    send_sem=far_send.at[index],
+                    recv_sem=far_recv.at[index],
                     device_id=(w, n),
                     device_id_type=MESH,
                 ).wait_recv()
 
     third = (third_ref[0], third_ref[1])
+    devices = wide * narrow
     momenta = third_ref.shape[1] // 2
-    depth = third_ref.shape[2]
-    for kt in range(per_kt):
-        value = halves(arrived[pl.ds(kt, depth, stride=per_kt), :])
-        turned[kt * 128 : (kt + 1) * 128, :] = dot3(third, value, ((1,), (0,))).T
-    for c in range(COMPS):
-        for k0 in range(ROWS):
-            value = turned[pl.ds(c * ROWS + k0, per_kt, stride=128), :]
-            out_ref[0, c, k0] = value[:, :momenta]
-            out_ref[1, c, k0] = value[:, momenta:]
+    start = lax.broadcasted_iota(jnp.int32, (devices, 128), 1) < over
+    for kt in range(0, per_kt, 2):
+        columns = []
+        for m in range(2):
+            real, imag, extra = [
+                arrived[pl.ds(part * per_kt + kt + m, devices, stride=block), :]
+                for part in range(3)
+            ]
+            real_one = jnp.where(start, pltpu.roll(real, over, 1), extra)
+            imag_one = jnp.where(start, pltpu.roll(imag, over, 1), pltpu.roll(extra, 64, 1))
+            columns.append(jnp.concatenate([real, imag, real_one, imag_one], axis=0))
+        value = dot3(third, halves(jnp.concatenate(columns, axis=1)), ((1,), (0,)))
+        for m in range(2):
+            whole = value[:, 128 * m : 128 * (m + 1)].T[:used]
+            out_ref[0, :, kt + m] = whole[:, :momenta].reshape(COMPS, ROWS, momenta)
+            out_ref[1, :, kt + m] = whole[:, momenta:].reshape(COMPS, ROWS, momenta)
     for copy in copies:
         copy.wait_send()
+
+
+def message_rows(per_kt):
+    return -(-3 * per_kt // 8) * 8
 
 
 def fused_body(wide, narrow, links, gauge):
@@ -526,26 +589,30 @@
     tables = make_tables(wide, narrow, slab_x)
     devices = wide * narrow
     per_kt = LT // narrow
-    block = 4 * per_kt
+    block = message_rows(per_kt)
     faces = 4 * HALF_SWEEPS + 2
     vmem = pl.BlockSpec(memory_space=pltpu.VMEM)
+    operands = [
+        links.reshape(4 * 4 * slab_x * 24, 128),
+        gauge.reshape(4 * slab_x * 24, 128),
+        *[jnp.asarray(table) for table in tables],
+    ]
     spectrum, field = pl.pallas_call(
         lambda *refs: fused(wide, narrow, *refs),
         out_shape=(
-            jax.ShapeDtypeStruct((2, COMPS, ROWS, per_kt, wide * slab_x * narrow), jnp.float32),
+            jax.ShapeDtypeStruct((2, COMPS, per_kt, ROWS, wide * slab_x * narrow), jnp.float32),
             jax.ShapeDtypeStruct((4 * slab_x * 24, 128), jnp.float32),
         ),
-        in_specs=[vmem, vmem, vmem, vmem, pl.BlockSpec(memory_space=pl.ANY), vmem],
+        in_specs=[pl.BlockSpec(memory_space=pl.ANY)] * len(operands),
         out_specs=(vmem, vmem),
         scratch_shapes=[
-            pltpu.VMEM(tables[2].shape, jnp.bfloat16),
+            *[pltpu.VMEM(value.shape, value.dtype) for value in operands],
             pltpu.VMEM((3 * HALF_SWEEPS + 1, 4, ROWS, LANES), jnp.float32),
             pltpu.VMEM((faces, 4, ROWS, LANES), jnp.float32),
             pltpu.VMEM((2, COMPS * ROWS, LANES), jnp.float32),
             pltpu.VMEM((devices * block, 128), jnp.float32),
             pltpu.VMEM((devices * block, 128), jnp.float32),
-            pltpu.VMEM((per_kt * 128, 128), jnp.float32),
-            pltpu.SemaphoreType.DMA,
+            pltpu.SemaphoreType.DMA((len(operands),)),
             pltpu.SemaphoreType.DMA((faces,)),
             pltpu.SemaphoreType.DMA((faces,)),
             pltpu.SemaphoreType.DMA((devices,)),
@@ -553,13 +620,10 @@
             pltpu.SemaphoreType.DMA,
         ],
         compiler_params=pltpu.CompilerParams(
-            collective_id=0, has_side_effects=True, vmem_limit_bytes=40 * 1024 * 1024
+            collective_id=0, has_side_effects=True, vmem_limit_bytes=VMEM_MIB * 1024 * 1024
         ),
-    )(
-        links.reshape(4 * 4 * slab_x * 24, 128),
-        gauge.reshape(4 * slab_x * 24, 128),
-        *[jnp.asarray(table) for table in tables],
-    )
+    )(*operands)
+    spectrum = jnp.transpose(spectrum, (0, 1, 3, 2, 4))
     return spectrum, field.reshape(gauge.shape)
 
 

time: 48.3 us -> 40.4 us (0.84)
  the two profiles are of different devices: /device:TPU:11 before, /device:TPU:0 now
where the time goes in v1:
time: 40.4 us; the launch traced here: 40.2 us
  Pallas kernels  36.5 us (90%)
  local copies, waits for them, and re-layouts  3.04 us (8%)
  between operations  0.65 us (2%)
    pallas_call x1, Pallas kernels, fused_body(): pl.pallas_call(lambda *refs: fused(wide, narrow, *refs), out_shape=(jax.S...  36.5 us
    unnamed x4, local copies, waits for them, and re-layouts  3.04 us

profile of v1, /device:TPU:0, one launch (start us, length us, event | category | flops | bytes accessed | tf_op | source)
XLA Modules:
  0.0 40.2 jit_solution(12289648529635992065)
XLA Ops:
  0.6 36.5 %shard_map.77 = (f32[2,12,12,8,64]{4,3,2,1,0:T(8,128)}, f32[192,128]{1,0:T(8,128)}) custom-call(f32[768,128]{1,0:T(8,128)} %bitcast.5, f32[192,128]{1,0:T(8,128)} %bitcast.6, bf16[2,256,96]{2,1,0:T(8,128)(2,1)} %constant.8.clone.refs_2_, f32[2,8,384]{2,1,0:T(8,128)} %constant.9.clone.refs_3_, bf16[2,768,768]{2,1,0:T(8,128)(2,1)} %constant.10.clone.refs_4_, ...), custom_call_target="tpu_custom_call" | custom-call | tf_op jit(solution)/shard_map/pallas_call | solution.py:600
  37.2 0.0 copy-start
  37.2 2.4 %copy.11 = f32[2,12,8,12,64]{4,2,3,1,0:T(8,128)} copy(f32[2,12,8,12,64]{4,2,3,1,0:T(8,128)} %bitcast.4) | data formatting | bytes 1179648
  39.6 0.0 copy-done
  39.6 0.6 %copy.12 = f32[4,2,1,3072]{3,2,1,0:T(1,128)} copy(f32[4,2,1,3072]{3,2,1,0:T(1,128)S(1)} %bitcast.7) | data formatting | bytes 196608
Async XLA Ops:
  37.2 2.4 %copy-start = (f32[192,128]{1,0:T(8,128)S(1)}, f32[192,128]{1,0:T(8,128)}, u32[]{:S(2)}) copy-start(f32[192,128]{1,0:T(8,128)} %get-tuple-element.5) | copy-start | bytes 294916

commit v2 on v1

--- a/solution.py
+++ b/solution.py
@@ -188,7 +188,7 @@
 INNER = LY // ROWS
 LANES = INNER * LT
 COMPS = 12
-VMEM_MIB = 60
+VMEM_MIB = 62
 MESH = pl.DeviceIdType.MESH
 
 
@@ -365,10 +365,10 @@
             lax.rem(my_n + step_n + narrow, narrow),
         )
 
-    def send_face(source, slot, step_w, step_n):
+    def send_face(source, slot, step_w, step_n, parts):
         copy = pltpu.make_async_remote_copy(
-            src_ref=face_out.at[source],
-            dst_ref=face_in.at[slot],
+            src_ref=face_out.at[source, pl.ds(0, parts)],
+            dst_ref=face_in.at[slot, pl.ds(0, parts)],
             send_sem=face_send.at[slot],
             recv_sem=face_recv.at[slot],
             device_id=neighbour(step_w, step_n),
@@ -383,6 +383,14 @@
 
     def got_face(slot):
         return [face_in[slot, a] for a in range(4)]
+
+    def put_packed(source, value, lanes):
+        for a in range(2):
+            face_out[source, a] = jnp.where(lanes, value[2 * a], behind_t(value[2 * a + 1]))
+
+    def got_packed(slot):
+        pairs = [face_in[slot, a] for a in range(2)]
+        return [v for pair in pairs for v in (pair, ahead_t(pair))]
 
     copies = []
     moved_links = None
@@ -391,30 +399,40 @@
         p = half % 2
         here = even if p == 0 else odd
         other = field[1 - p]
-        moved_links = [qmul(other, link[1 - p][mu]) for mu in range(4)]
-        put_face(3 * half, other)
-        put_face(3 * half + 1, moved_links[0])
-        put_face(3 * half + 2, moved_links[2])
+        away = odd if p == 0 else even
+        source, slot = 4 * half, 4 * half
+        put_packed(source, other, away)
+        moved_x = qmul(other, link[1 - p][0])
+        put_packed(source + 1, moved_x, here)
+        put_face(source + 2, other)
         if half == 0:
             pl.semaphore_wait(barrier, wide * narrow - 1)
         started = [
-            send_face(3 * half, 4 * half, -1, 0),
-            send_face(3 * half, 4 * half + 1, 0, -1),
-            send_face(3 * half + 1, 4 * half + 2, 1, 0),
-            send_face(3 * half + 2, 4 * half + 3, 0, 1),
+            send_face(source, slot, -1, 0, 2),
+            send_face(source + 1, slot + 2, 1, 0, 2),
+            send_face(source + 2, slot + 1, 0, -1, 4),
+        ]
+        moved_z = qmul(other, link[1 - p][2])
+        put_face(source + 3, moved_z)
+        started.append(send_face(source + 3, slot + 3, 0, 1, 4))
+        moved_links = [
+            moved_x, qmul(other, link[1 - p][1]), moved_z, qmul(other, link[1 - p][3])
         ]
         copies += started
         total = qmul([ahead_y(v) for v in other], qconj(link[p][1]))
         total = qadd(total, [behind_y(v) for v in moved_links[1]])
         total = qadd(total, qmul([ahead_t(v) for v in other], qconj(link[p][3])))
         total = qadd(total, [behind_t(v) for v in moved_links[3]])
-        for copy in started:
-            copy.wait_recv()
-        kept_x, kept_z = got_face(4 * half), got_face(4 * half + 1)
+        started[2].wait_recv()
+        kept_z = got_face(slot + 1)
+        total = qadd(total, qmul(kept_z, qconj(link[p][2])))
+        started[3].wait_recv()
+        total = qadd(total, got_face(slot + 3))
+        started[0].wait_recv()
+        kept_x = got_packed(slot)
         total = qadd(total, qmul(qwhere(here, other, kept_x), qconj(link[p][0])))
-        total = qadd(total, qmul(kept_z, qconj(link[p][2])))
-        total = qadd(total, qwhere(here, got_face(4 * half + 2), moved_links[0]))
-        total = qadd(total, got_face(4 * half + 3))
+        started[1].wait_recv()
+        total = qadd(total, qwhere(here, got_packed(slot + 2), moved_links[0]))
         centre = field[p]
         relaxed = [OMEGA * v for v in qmul(total, qconj(centre))]
         relaxed[0] = relaxed[0] + (1.0 - OMEGA) * qnorm(total)
@@ -422,9 +440,11 @@
         field[p] = [v / bound for v in qmul(relaxed, centre)]
 
     p = (HALF_SWEEPS - 1) % 2
-    source, slot = 3 * HALF_SWEEPS, 4 * HALF_SWEEPS
-    put_face(source, field[p])
-    started = [send_face(source, slot, -1, 0), send_face(source, slot + 1, 0, -1)]
+    here = even if p == 0 else odd
+    source, slot = 4 * HALF_SWEEPS, 4 * HALF_SWEEPS
+    put_packed(source, field[p], here)
+    put_face(source + 1, field[p])
+    started = [send_face(source, slot, -1, 0, 2), send_face(source + 1, slot + 1, 0, -1, 4)]
     copies += started
     for a in range(4):
         zero = jnp.where(even, field[0][a], field[1][a])
@@ -437,7 +457,6 @@
     carried = [None, None]
     carried[1 - p] = moved_links
     carried[p] = [qmul(field[p], link[p][mu]) for mu in range(4)]
-    here = even if p == 0 else odd
 
     def put_potential(mu, ahead):
         value = [qmul(carried[q][mu], qconj(ahead[q])) for q in range(2)]
@@ -450,16 +469,16 @@
 
     put_potential(1, [[ahead_y(v) for v in field[1 - q]] for q in range(2)])
     put_potential(3, [[ahead_t(v) for v in field[1 - q]] for q in range(2)])
-    for copy in started:
-        copy.wait_recv()
-    fresh_x, fresh_z = got_face(slot), got_face(slot + 1)
+    started[1].wait_recv()
+    fresh_z = got_face(slot + 1)
+    put_potential(2, [[kept_z, fresh_z][q != p] for q in range(2)])
+    started[0].wait_recv()
+    fresh_x = got_packed(slot)
     there = odd if p == 0 else even
     ahead = [None, None]
     ahead[p] = qwhere(here, field[1 - p], kept_x)
     ahead[1 - p] = qwhere(there, field[p], fresh_x)
     put_potential(0, ahead)
-    ahead[p], ahead[1 - p] = kept_z, fresh_z
-    put_potential(2, ahead)
 
     loads[2].wait()
     loads[3].wait()
@@ -607,7 +626,7 @@
         out_specs=(vmem, vmem),
         scratch_shapes=[
             *[pltpu.VMEM(value.shape, value.dtype) for value in operands],
-            pltpu.VMEM((3 * HALF_SWEEPS + 1, 4, ROWS, LANES), jnp.float32),
+            pltpu.VMEM((faces, 4, ROWS, LANES), jnp.float32),
             pltpu.VMEM((faces, 4, ROWS, LANES), jnp.float32),
             pltpu.VMEM((2, COMPS * ROWS, LANES), jnp.float32),
             pltpu.VMEM((devices * block, 128), jnp.float32),

time: 40.4 us -> 39.6 us (0.980)
  Pallas kernels: 36.5 us -> 35.7 us
    pallas_call x1, Pallas kernels: 36.5 us -> 35.7 us  [fused_body(): pl.pallas_call(lambda *refs: fused(wide, narrow, *refs), out_shape=(jax.S...]
where the time goes in v2:
time: 39.6 us; the launch traced here: 39.4 us
  Pallas kernels  35.7 us (90%)
  local copies, waits for them, and re-layouts  3.04 us (8%)
  between operations  0.65 us (2%)
    pallas_call x1, Pallas kernels, fused_body(): pl.pallas_call(lambda *refs: fused(wide, narrow, *refs), out_shape=(jax.S...  35.7 us
    unnamed x4, local copies, waits for them, and re-layouts  3.04 us

profile of v2, /device:TPU:0, one launch (start us, length us, event | category | flops | bytes accessed | tf_op | source)
XLA Modules:
  0.0 39.4 jit_solution(6821087279379672793)
XLA Ops:
  0.6 35.7 %shard_map.77 = (f32[2,12,12,8,64]{4,3,2,1,0:T(8,128)}, f32[192,128]{1,0:T(8,128)}) custom-call(f32[768,128]{1,0:T(8,128)} %bitcast.5, f32[192,128]{1,0:T(8,128)} %bitcast.6, bf16[2,256,96]{2,1,0:T(8,128)(2,1)} %constant.8.clone.refs_2_, f32[2,8,384]{2,1,0:T(8,128)} %constant.9.clone.refs_3_, bf16[2,768,768]{2,1,0:T(8,128)(2,1)} %constant.10.clone.refs_4_, ...), custom_call_target="tpu_custom_call" | custom-call | tf_op jit(solution)/shard_map/pallas_call | solution.py:619
  36.4 0.0 copy-start
  36.4 2.4 %copy.11 = f32[2,12,8,12,64]{4,2,3,1,0:T(8,128)} copy(f32[2,12,8,12,64]{4,2,3,1,0:T(8,128)} %bitcast.4) | data formatting | bytes 1179648
  38.8 0.0 copy-done
  38.8 0.6 %copy.12 = f32[4,2,1,3072]{3,2,1,0:T(1,128)} copy(f32[4,2,1,3072]{3,2,1,0:T(1,128)S(1)} %bitcast.7) | data formatting | bytes 196608
Async XLA Ops:
  36.4 2.4 %copy-start = (f32[192,128]{1,0:T(8,128)S(1)}, f32[192,128]{1,0:T(8,128)}, u32[]{:S(2)}) copy-start(f32[192,128]{1,0:T(8,128)} %get-tuple-element.5) | copy-start | bytes 294916

commit v3 on v2

--- a/solution.py
+++ b/solution.py
@@ -513,7 +513,7 @@
     my_z, my_x = my_w // pair, lax.rem(my_w, pair)
 
     def span(w, n):
-        return pl.ds(pl.multiple_of((w * narrow + n) * block, 8), block)
+        return pl.ds(pl.multiple_of((w * narrow + n) * block, 8), 3 * per_kt)
 
     mine = span(my_w, my_n)
     steps = sorted(range(groups), key=lambda step: -min(step, groups - step))
@@ -541,7 +541,7 @@
                 w, n = group * pair + x, lax.rem(my_n + k, narrow)
                 index = (step * pair + q) * narrow + k
                 held = pl.ds(
-                    pl.multiple_of(((place * pair + x) * narrow + n) * block, 8), block
+                    pl.multiple_of(((place * pair + x) * narrow + n) * block, 8), 3 * per_kt
                 )
                 if index == 0:
                     own = pltpu.make_async_copy(outgoing.at[held], arrived.at[mine], own_sem)
@@ -568,7 +568,7 @@
                 w = lax.rem(my_z + groups - step, groups) * pair + lax.rem(my_x + q, pair)
                 n = lax.rem(my_n + narrow - k, narrow)
                 pltpu.make_async_remote_copy(
-                    src_ref=outgoing.at[pl.ds(0, block)],
+                    src_ref=outgoing.at[pl.ds(0, 3 * per_kt)],
                     dst_ref=arrived.at[span(w, n)],
                     send_sem=far_send.at[index],
                     recv_sem=far_recv.at[index],

time: 39.6 us -> 38.4 us (0.970)
  Pallas kernels: 35.7 us -> 34.5 us
    pallas_call x1, Pallas kernels: 35.7 us -> 34.5 us  [fused_body(): pl.pallas_call(lambda *refs: fused(wide, narrow, *refs), out_shape=(jax.S...]
where the time goes in v3:
time: 38.4 us; the launch traced here: 38.2 us
  Pallas kernels  34.5 us (90%)
  local copies, waits for them, and re-layouts  3.04 us (8%)
  between operations  0.65 us (2%)
    pallas_call x1, Pallas kernels, fused_body(): pl.pallas_call(lambda *refs: fused(wide, narrow, *refs), out_shape=(jax.S...  34.5 us
    unnamed x4, local copies, waits for them, and re-layouts  3.04 us

profile of v3, /device:TPU:0, one launch (start us, length us, event | category | flops | bytes accessed | tf_op | source)
XLA Modules:
  0.0 38.2 jit_solution(13595784140203660302)
XLA Ops:
  0.6 34.5 %shard_map.77 = (f32[2,12,12,8,64]{4,3,2,1,0:T(8,128)}, f32[192,128]{1,0:T(8,128)}) custom-call(f32[768,128]{1,0:T(8,128)} %bitcast.5, f32[192,128]{1,0:T(8,128)} %bitcast.6, bf16[2,256,96]{2,1,0:T(8,128)(2,1)} %constant.8.clone.refs_2_, f32[2,8,384]{2,1,0:T(8,128)} %constant.9.clone.refs_3_, bf16[2,768,768]{2,1,0:T(8,128)(2,1)} %constant.10.clone.refs_4_, ...), custom_call_target="tpu_custom_call" | custom-call | tf_op jit(solution)/shard_map/pallas_call | solution.py:619
  35.2 0.0 copy-start
  35.2 2.4 %copy.11 = f32[2,12,8,12,64]{4,2,3,1,0:T(8,128)} copy(f32[2,12,8,12,64]{4,2,3,1,0:T(8,128)} %bitcast.4) | data formatting | bytes 1179648
  37.6 0.0 copy-done
  37.6 0.6 %copy.12 = f32[4,2,1,3072]{3,2,1,0:T(1,128)} copy(f32[4,2,1,3072]{3,2,1,0:T(1,128)S(1)} %bitcast.7) | data formatting | bytes 196608
Async XLA Ops:
  35.2 2.4 %copy-start = (f32[192,128]{1,0:T(8,128)S(1)}, f32[192,128]{1,0:T(8,128)}, u32[]{:S(2)}) copy-start(f32[192,128]{1,0:T(8,128)} %get-tuple-element.5) | copy-start | bytes 294916
